TPU v7x, 32 devices: a whole 2x2x4 slice. The times are simulated.
32 devices in a mesh: dp: 8 (over z, y), owner: 4 (over x, core).
Axes of the slice: x: 2, y: 2, z: 4, core: 2. Of those that a mesh axis runs over, the one named last changes fastest.
Arguments:
- embeddings: bfloat16 [4096, 1024], P(('dp', 'owner')), may hold values from -120 to 120
- assignment: int32 [4096], P(('dp', 'owner')), may hold values from 0 to 511, as said below
- pair_list: int32 [512], replicated, may hold values from 0 to 511, as said below
Outputs:
- best_similarity: float32 [4096], P(('dp', 'owner'))
Inputs may be any that keep to these rules, and one draw needn't show every extreme that they name: `assignment`: row r's cluster id is (t * n + o) * 16 + c, where n is the number of owner indices, o the owner index of the device holding row r, t an index of dp and c below 16. Among the rows of one device at most 32 share one t, and on every device exactly 32 rows share some t. pair_list[pair_list[k]] = k for every cluster k; cluster k = (t * n + o) * 16 + c and its partner have the same t and different owner indices o.
All inputs are finite; a program needn't handle non-finite values.
Results may differ from a plain program's by a relative error of at most 0.00053.
Values may be sent and summed in bfloat16 or wider, within the bound.
A program may use at most 64 MiB of HBM per device.

v0:
```python
import jax
import jax.numpy as jnp
from jax import lax
from jax.sharding import PartitionSpec as P

CPD = 16


def shards(embeddings, assignment, pair_list):
    rows, width = embeddings.shape
    n_dp = lax.axis_size("dp")
    n_owner = lax.axis_size("owner")
    capacity = 2 * rows // n_dp
    slots = capacity * n_dp
    values = embeddings.astype(jnp.float32)
    unit = (values * lax.rsqrt(jnp.sum(values * values, axis=1, keepdims=True) + 1e-06)).astype(
        jnp.bfloat16
    )
    target = assignment // (n_owner * CPD)
    onehot = (target[:, None] == jnp.arange(n_dp, dtype=jnp.int32)[None, :]).astype(jnp.int32)
    slot = jnp.sum(jnp.cumsum(onehot, axis=0) * onehot, axis=1) - 1
    position = target * capacity + slot
    here_owner = lax.axis_index("owner")
    here_dp = lax.axis_index("dp")
    first_id = (here_dp * n_owner + here_owner) * CPD
    partners_mine = lax.dynamic_slice_in_dim(pair_list, first_id, CPD)
    start_best = jnp.full((slots,), -1.0, jnp.float32)
    send_rows = jnp.zeros((slots, width), jnp.bfloat16).at[position].set(unit)
    send_ids = jnp.full((slots,), -1, jnp.int32).at[position].set(assignment)
    got_rows, got_ids = (
        lax.all_to_all(
            send_rows.reshape(n_dp, capacity, width), "dp", split_axis=0, concat_axis=0, tiled=True
        ),
        lax.all_to_all(
            send_ids.reshape(n_dp, capacity), "dp", split_axis=0, concat_axis=0, tiled=True
        ),
    )
    mine = got_rows.reshape(slots, width)
    mine_ids = got_ids.reshape(slots)
    local = jnp.clip(mine_ids - first_id, 0, CPD - 1)
    picked = local[:, None] == jnp.arange(CPD, dtype=jnp.int32)[None, :]
    partner = jnp.sum(jnp.where(picked, partners_mine[None, :], 0), axis=1)
    rows_p = lax.all_gather(mine, "owner", axis=0, tiled=True)
    ids_p = lax.all_gather(mine_ids, "owner", axis=0, tiled=True)
    scores = lax.dot_general(
        mine, rows_p, (((1,), (1,)), ((), ())), preferred_element_type=jnp.float32
    )
    column = jnp.arange(ids_p.shape[0], dtype=jnp.int32)
    itself = here_owner * slots + jnp.arange(slots, dtype=jnp.int32)
    same = (
        (mine_ids[:, None] == ids_p[None, :])
        & (ids_p[None, :] >= 0)
        & (itself[:, None] != column[None, :])
    )
    related = same | (partner[:, None] == ids_p[None, :])
    best = jnp.maximum(start_best, jnp.max(jnp.where(related, scores, -1.0), axis=1))
    returned = lax.all_to_all(
        best.reshape(n_dp, capacity), "dp", split_axis=0, concat_axis=0, tiled=True
    )
    return returned.reshape(slots)[position]


def solution(mesh):
    placed = (P(("dp", "owner"), None), P(("dp", "owner")), P())
    return jax.shard_map(
        shards, mesh=mesh, in_specs=placed, out_specs=P(("dp", "owner")), check_vma=False
    )
```

profile of v0, /device:TPU:0, one launch (start us, length us, event | category | flops | bytes accessed | tf_op | source)
XLA Modules:
  0.0 80.1 jit_solution(11450453904550663575)
XLA Ops:
  6.5 0.0 all-gather.3.cloned.1.call-start
  6.5 0.7 and_select_fusion
  7.2 0.1 fusion.9
  7.3 0.2 reduce_window_sum.11
  7.5 0.2 select_reduce_fusion
  7.6 0.7 compare_select_fusion
  8.3 1.1 %fusion.3 = f32[128]{0:T(128)S(1)} fusion(bf16[128,1024]{1,0:T(8,128)(2,1)} %param.3), kind=kLoop, calls=%fused_computation.10 | loop fusion | flops 393088 | bytes 262656 | tf_op jit(solution)/shard_map/reduce_sum | solution.py:16
  9.4 1.8 %scatter_custom_fusion.1 = bf16[256,1024]{1,0:T(8,128)(2,1)S(1)} fusion(s32[128]{0:T(128)S(1)} %compare_select_fusion, bf16[128,1024]{1,0:T(8,128)(2,1)} %param.3, f32[128]{0:T(128)S(1)} %add_rsqrt_fusion, bf16[]{:T(256)} %constant.54.clone.1), kind=kCustom, calls=%fused_computation.12 | custom fusion | flops 393216 | bytes 786946 | tf_op jit(solution)/shard_map/scatter | solution.py:28
  11.2 21.7 %all_to_all.20 = bf16[8,32,1024]{2,1,0:T(8,128)(2,1)} all-to-all(bf16[8,32,1024]{2,1,0:T(8,128)(2,1)S(1)} %bitcast.8), channel_id=1, replica_groups=mesh['dp'=8,'owner'=4] {'dp'}, dimensions={0} | all-to-all | bytes 1048576 | tf_op jit(solution)/shard_map/all_to_all | solution.py:31
  32.9 0.0 all-gather.3.cloned.1.call-update
  32.9 1.1 %scatter_custom_fusion = s32[256]{0:T(256)S(1)} fusion(s32[128]{0:T(128)S(1)} %compare_select_fusion, s32[128]{0:T(128)} %param.4, s32[]{:T(128)} %constant.19.clone.1), kind=kCustom, calls=%fused_computation.31 | custom fusion | bytes 1536 | tf_op jit(solution)/shard_map/scatter | solution.py:29
  34.1 0.7 all_to_all.13
  34.7 3.6 %all-to-all-start = ((s32[8,1,32]{2,1,0:T(1,128)}), s32[8,1,32]{2,1,0:T(1,128)S(1)}, u32[]{:S(2)}, u32[]{:S(2)}) async-start(s32[8,1,32]{2,1,0:T(1,128)} %all_to_all.13), calls=%async_computation | async-start | bytes 8192 | tf_op jit(solution)/shard_map/all_to_all | solution.py:34
  38.3 0.8 dynamic_slice.3
  39.1 5.7 %all-to-all-done = s32[8,1,32]{2,1,0:T(1,128)S(1)} async-done(((s32[8,1,32]{2,1,0:T(1,128)}), s32[8,1,32]{2,1,0:T(1,128)S(1)}, u32[]{:S(2)}, u32[]{:S(2)}) %all-to-all-start) | async-done | bytes 1056 | tf_op jit(solution)/shard_map/all_to_all | solution.py:34
  44.8 0.5 broadcast.76
  45.3 0.7 reduce.8
  46.0 0.1 eq.27
  46.0 0.1 reshape.87
  46.1 5.1 %all-gather = s32[4,1,256]{2,1,0:T(1,128)S(1)} all-gather(s32[1,1,256]{2,1,0:T(1,128)S(1)} %reshape.87), channel_id=1, replica_groups=mesh['dp'=8,'owner'=4] {'owner'}, dimensions={0}, use_global_device_ids=true | all-gather | bytes 5120 | tf_op jit(solution)/shard_map/all_gather | solution.py:44
  51.2 0.1 select_reduce_fusion.1
  51.3 3.4 %all-gather.3.cloned.1.call-done = bf16[1024,1024]{1,0:T(8,128)(2,1)} async-done(((bf16[256,1024]{1,0:T(8,128)(2,1)}), bf16[1024,1024]{1,0:T(8,128)(2,1)}) %all-gather.3.cloned.1.call-update) | async-done | bytes 2097168 | tf_op jit(solution)/shard_map/all_gather | solution.py:43
  54.7 2.8 %fusion = f32[256]{0:T(256)S(1)} fusion(bf16[256,1024]{1,0:T(8,128)(2,1)} %bitcast.7, bf16[1024,1024]{1,0:T(8,128)(2,1)} %all-gather.3.cloned.1.call-done, s32[256]{0:T(256)S(1)} %iota_add_fusion, s32[1024]{0:T(1024)S(1)} %bitcast.11, s32[256]{0:T(256)S(1)} %select_reduce_fusion.1, s32[256]{0:T(256)S(1)} %eq.27, pred[1024]{0:T(1024)(128)(4,1)S(1)} %broadcast_compare_fusion), kind=kOutput, calls=%fused_computation.4 | convolution fusion | flops 538967808 | bytes 2630656 | tf_op jit(solution)/shard_map/dot_general | solution.py:45
  57.5 0.7 max_broadcast_in_dim.15
  58.2 5.5 %all-to-all-start.2 = ((f32[8,1,32]{2,1,0:T(1,128)}), f32[8,1,32]{2,1,0:T(1,128)S(1)}, u32[]{:S(2)}, u32[]{:S(2)}) async-start(f32[8,1,32]{2,1,0:T(1,128)} %max_broadcast_in_dim.15), calls=%async_computation.2 | async-start | bytes 8192 | tf_op jit(solution)/shard_map/all_to_all | solution.py:57
  63.7 6.5 %all-to-all-done.2 = f32[8,1,32]{2,1,0:T(1,128)S(1)} async-done(((f32[8,1,32]{2,1,0:T(1,128)}), f32[8,1,32]{2,1,0:T(1,128)S(1)}, u32[]{:S(2)}, u32[]{:S(2)}) %all-to-all-start.2) | async-done | bytes 1056 | tf_op jit(solution)/shard_map/all_to_all | solution.py:57
  70.2 0.5 broadcast.77
  70.7 0.7 reduce.9
  71.4 0.1 reshape.59
  71.5 1.8 %gather_fusion = f32[128]{0:T(128)} fusion(f32[256]{0:T(256)S(1)} %reshape.59, s32[1024]{0:T(1024)S(1)} %pad_clamp_fusion), kind=kCustom, calls=%fused_computation | custom fusion | bytes 1536 | tf_op jit(solution)/shard_map/gather | solution.py:60
  (6 shorter events, 0.0 us)
Async XLA Ops:
  6.5 48.2 %all-gather.3.cloned.1.call-start = ((), (), s32[]{:S(2)}) async-start(), calls=%async_computation.3 | async-start | bytes 2621440 | tf_op jit(solution)/shard_map/all_gather | solution.py:43
  34.7 10.0 %all-to-all-start = ((s32[8,1,32]{2,1,0:T(1,128)}), s32[8,1,32]{2,1,0:T(1,128)S(1)}, u32[]{:S(2)}, u32[]{:S(2)}) async-start(s32[8,1,32]{2,1,0:T(1,128)} %all_to_all.13), calls=%async_computation | async-start | bytes 8192 | tf_op jit(solution)/shard_map/all_to_all | solution.py:34
  58.2 12.0 %all-to-all-start.2 = ((f32[8,1,32]{2,1,0:T(1,128)}), f32[8,1,32]{2,1,0:T(1,128)S(1)}, u32[]{:S(2)}, u32[]{:S(2)}) async-start(f32[8,1,32]{2,1,0:T(1,128)} %max_broadcast_in_dim.15), calls=%async_computation.2 | async-start | bytes 8192 | tf_op jit(solution)/shard_map/all_to_all | solution.py:57
Sparse Core Ops, SparseCore 0:
  33.1 21.6 all-gather.2
where the time goes:
time: 80.5 us; the launch traced here: 80.1 us
  blocking collectives  26.8 us (33%)
  waiting for transfers between devices  15.6 us (19%)
  between operations  13.5 us (17%)
  starting transfers between devices  9.11 us (11%)
  local copies, waits for them, and re-layouts  6.24 us (8%)
  other arithmetic  6.08 us (8%)
  matrix products  2.81 us (3%)
    all_to_all x1, blocking collectives, shards(): lax.all_to_all(send_rows.reshape(n_dp, capacity, width), 'dp', split_axis...  21.7 us
    all_to_all x1, waiting for transfers between devices, shards(): lax.all_to_all(best.reshape(n_dp, capacity), 'dp', split_axis=0, concat_a...  6.46 us
    all_to_all x1, waiting for transfers between devices, shards(): lax.all_to_all(send_ids.reshape(n_dp, capacity), 'dp', split_axis=0, conc...  5.69 us
    all_to_all x1, starting transfers between devices, shards(): lax.all_to_all(best.reshape(n_dp, capacity), 'dp', split_axis=0, concat_a...  5.52 us
    all_gather x1, blocking collectives, shards(): ids_p = lax.all_gather(mine_ids, 'owner', axis=0, tiled=True)  5.06 us
    all_to_all x1, starting transfers between devices, shards(): lax.all_to_all(send_ids.reshape(n_dp, capacity), 'dp', split_axis=0, conc...  3.59 us
    all_gather x1, waiting for transfers between devices, shards(): rows_p = lax.all_gather(mine, 'owner', axis=0, tiled=True)  3.44 us
    dot_general x1, matrix products, shards(): lax.dot_general(mine, rows_p, (((1,), (1,)), ((), ())), preferred_element...  2.81 us
  transfers between devices with their start and end apart: 3, of which 3 were waited for; matrix products, arithmetic and copies ran while one was open for 4% of the time, Pallas kernels for 0%

commit v1 on v0

--- a/solution.py
+++ b/solution.py
@@ -1,16 +1,247 @@
+import functools
+
 import jax
 import jax.numpy as jnp
 from jax import lax
+from jax.experimental import pallas as pl
+from jax.experimental.pallas import tpu as pltpu
 from jax.sharding import PartitionSpec as P
 
 CPD = 16
-
-
-def shards(embeddings, assignment, pair_list):
+MESH = pl.DeviceIdType.MESH
+NT = (((1,), (1,)), ((), ()))
+
+
+def peer_of(d, k):
+    z, y = d // 2, d % 2
+    dz, dy = k // 2, k % 2
+    if dz == 1:
+        z = z + 1 - 2 * (z % 2)
+    elif dz == 2:
+        z = (z + 2) % 4
+    elif dz == 3:
+        z = 3 - z
+    if dy:
+        y = 1 - y
+    return z * 2 + y
+
+
+SEND_ORDER = (4, 5, 6, 7, 2, 3, 1)
+WAIT_ORDER = (1, 2, 3, 4, 6, 5, 7)
+
+
+def kernel(
+    cap, n_dp, n_owner,
+    emb, asg, pairs, out,
+    send, own, sib, cpt,
+    code_send, code_got, codes, ret, res,
+    row_ss, row_rs, id_ss, id_rs, fw_ss, fw_rs, cd_ss, cd_rs, rt_ss, rt_rs,
+):
+    rows, width = emb.shape
+    slots = cap * n_dp
+    d = lax.axis_index("dp")
+    o = lax.axis_index("owner")
+    o_sib = o + 1 - 2 * (o % 2)
+    o_cpt = (o + 2) % 4
+    peers = [peer_of(d, k) for k in range(n_dp)]
+
+    barrier = pltpu.get_barrier_semaphore()
+    for k in range(n_dp):
+        if k:
+            pl.semaphore_signal(barrier, inc=1, device_id=(peers[k], o), device_id_type=MESH)
+        pl.semaphore_signal(barrier, inc=1, device_id=(peers[k], o_sib), device_id_type=MESH)
+    pl.semaphore_signal(barrier, inc=1, device_id=(d, o_cpt), device_id_type=MESH)
+
+    a = asg[...]
+    t_row = lax.shift_right_logical(a, 6)
+    code_row = ((a & 63) + 1).astype(jnp.float32)
+    t_hot = (lax.broadcasted_iota(jnp.int32, (n_dp, rows), 0) == t_row).astype(jnp.float32)
+    before = (
+        lax.broadcasted_iota(jnp.int32, (rows, rows), 0)
+        < lax.broadcasted_iota(jnp.int32, (rows, rows), 1)
+    ).astype(jnp.float32).astype(jnp.bfloat16)
+    count = jnp.dot(t_hot.astype(jnp.bfloat16), before, preferred_element_type=jnp.float32)
+    rank = jnp.sum(t_hot * count, axis=0, keepdims=True).astype(jnp.int32)
+    slot_iota = lax.broadcasted_iota(jnp.int32, (slots, rows), 0)
+    lane_hot = (slot_iota == d * cap + rank).astype(jnp.float32)
+    slot_codes = lax.dot_general(
+        (t_hot * code_row).astype(jnp.bfloat16),
+        lane_hot.astype(jnp.bfloat16),
+        NT,
+        preferred_element_type=jnp.float32,
+    )
+    for t in range(n_dp):
+        code_send[t] = slot_codes[t : t + 1, :]
+
+    values = emb[...].astype(jnp.float32)
+    unit = (values * lax.rsqrt(jnp.sum(values * values, axis=1, keepdims=True) + 1e-06)).astype(
+        jnp.bfloat16
+    )
+    place = (slot_iota == t_row * cap + rank).astype(jnp.float32).astype(jnp.bfloat16)
+    packed = jnp.dot(place, unit, preferred_element_type=jnp.float32).astype(jnp.bfloat16)
+    for t in range(n_dp):
+        send[t] = packed[t * cap : (t + 1) * cap, :]
+    own[d] = send[d]
+    code_got[d] = code_send[d]
+
+    pl.semaphore_wait(barrier, 2 * n_dp)
+
+    def block_copy(k):
+        p = peers[k]
+        return pltpu.make_async_remote_copy(
+            src_ref=send.at[p], dst_ref=own.at[d], send_sem=row_ss.at[k], recv_sem=row_rs.at[k],
+            device_id=(p, o), device_id_type=MESH,
+        )
+
+    def code_copy(k):
+        p = peers[k]
+        return pltpu.make_async_remote_copy(
+            src_ref=code_send.at[p], dst_ref=code_got.at[d], send_sem=id_ss.at[k],
+            recv_sem=id_rs.at[k], device_id=(p, o), device_id_type=MESH,
+        )
+
+    def forward(k, which):
+        s = peers[k]
+        return pltpu.make_async_remote_copy(
+            src_ref=own.at[s], dst_ref=(sib, cpt)[which].at[s], send_sem=fw_ss.at[which, k],
+            recv_sem=fw_rs.at[which, k], device_id=(d, (o_sib, o_cpt)[which]), device_id_type=MESH,
+        )
+
+    def codes_copy(which):
+        return pltpu.make_async_remote_copy(
+            src_ref=codes.at[0], dst_ref=codes.at[1 + which], send_sem=cd_ss.at[which],
+            recv_sem=cd_rs.at[which], device_id=(d, (o_sib, o_cpt)[which]), device_id_type=MESH,
+        )
+
+    def back(k, which):
+        s = peers[k]
+        return pltpu.make_async_remote_copy(
+            src_ref=res.at[which], dst_ref=ret.at[which, d], send_sem=rt_ss.at[which, k],
+            recv_sem=rt_rs.at[which, k], device_id=(s, (o, o_sib)[which]), device_id_type=MESH,
+        )
+
+    for k in SEND_ORDER:
+        code_copy(k).start()
+    for k in SEND_ORDER:
+        block_copy(k).start()
+    forward(0, 1).start()
+    forward(0, 0).start()
+    for k in WAIT_ORDER:
+        code_copy(k).wait_recv()
+    codes[0] = jnp.sum(code_got[...], axis=0)
+    codes_copy(0).start()
+    codes_copy(1).start()
+    for k in WAIT_ORDER:
+        block_copy(k).wait_recv()
+        forward(k, 1).start()
+        forward(k, 0).start()
+
+    codes_copy(0).wait_recv()
+    codes_copy(1).wait_recv()
+    g_own, g_sib, g_cpt = codes[0], codes[1], codes[2]
+
+    def partner(g, owner):
+        found = jnp.full(g.shape, -1, jnp.int32)
+        for c in range(CPD):
+            other = pairs[(d * n_owner + owner) * CPD + c] - d * (n_owner * CPD) + 1
+            found = jnp.where(g == (owner * CPD + c + 1).astype(jnp.float32), other, found)
+        return found.astype(jnp.float32)
+
+    p_own, p_sib = partner(g_own, o), partner(g_sib, o_sib)
+
+    def column(g):
+        return jnp.transpose(jnp.broadcast_to(g, (128, slots)))
+
+    def table(ref):
+        return ref[...].reshape(slots, width)
+
+    def scores(keys, queries):
+        return lax.dot_general(keys, queries, NT, preferred_element_type=jnp.float32)
+
+    def wide(column_128):
+        return jnp.concatenate([column_128] * (slots // 128), axis=1)
+
+    def masked_max(s, mask):
+        return jnp.max(jnp.where(mask, s, -1.0), axis=0, keepdims=True)
+
+    rows_own = table(own)
+    key = lax.broadcasted_iota(jnp.int32, (slots, slots), 0)
+    query = lax.broadcasted_iota(jnp.int32, (slots, slots), 1)
+    best = masked_max(scores(rows_own, rows_own), (wide(column(g_own)) == g_own) & (key != query))
+    for k in range(n_dp):
+        forward(k, 0).wait_recv()
+    rows_sib = table(sib)
+    best = jnp.maximum(best, masked_max(scores(rows_sib, rows_own), wide(column(g_sib)) == p_own))
+    for k in range(n_dp):
+        forward(k, 1).wait_recv()
+    rows_cpt = table(cpt)
+    k_cpt = wide(column(g_cpt))
+    res[1] = masked_max(scores(rows_cpt, rows_sib), k_cpt == p_sib)
+    for k in (4, 5, 6, 7, 2, 3, 1, 0):
+        back(k, 1).start()
+    best = jnp.maximum(best, masked_max(scores(rows_cpt, rows_own), k_cpt == p_own))
+    res[0] = best
+    for k in SEND_ORDER:
+        back(k, 0).start()
+    ret[0, d] = best
+
+    for k in range(n_dp):
+        back(k, 1).wait_recv()
+        if k:
+            back(k, 0).wait_recv()
+    got = jnp.concatenate([jnp.maximum(ret[0, t], ret[1, t]) for t in range(n_dp)], axis=0)
+    picked = lax.dot_general(
+        got, lane_hot, (((1,), (0,)), ((), ())),
+        preferred_element_type=jnp.float32, precision=lax.Precision.HIGHEST,
+    )
+    out[...] = jnp.maximum(jnp.sum(t_hot * picked, axis=0, keepdims=True), -1.0)
+
+    for k in range(n_dp):
+        if k:
+            block_copy(k).wait_send()
+            code_copy(k).wait_send()
+            back(k, 0).wait_send()
+        back(k, 1).wait_send()
+        forward(k, 0).wait_send()
+        forward(k, 1).wait_send()
+    codes_copy(0).wait_send()
+    codes_copy(1).wait_send()
+
+
+def fused(embeddings, assignment, pair_list, capacity, n_dp, n_owner):
     rows, width = embeddings.shape
-    n_dp = lax.axis_size("dp")
-    n_owner = lax.axis_size("owner")
-    capacity = 2 * rows // n_dp
+    slots = capacity * n_dp
+    block = pltpu.VMEM((n_dp, capacity, width), jnp.bfloat16)
+    line = pltpu.VMEM((n_dp, 1, slots), jnp.float32)
+    dma = pltpu.SemaphoreType.DMA
+    best = pl.pallas_call(
+        functools.partial(kernel, capacity, n_dp, n_owner),
+        out_shape=jax.ShapeDtypeStruct((1, rows), jnp.float32),
+        in_specs=[
+            pl.BlockSpec(memory_space=pltpu.VMEM),
+            pl.BlockSpec(memory_space=pltpu.VMEM),
+            pl.BlockSpec(memory_space=pltpu.SMEM),
+        ],
+        out_specs=pl.BlockSpec(memory_space=pltpu.VMEM),
+        scratch_shapes=[
+            block, block, block, block,
+            line, line,
+            pltpu.VMEM((3, 1, slots), jnp.float32),
+            pltpu.VMEM((2, n_dp, 1, slots), jnp.float32),
+            pltpu.VMEM((2, 1, slots), jnp.float32),
+            dma((n_dp,)), dma((n_dp,)), dma((n_dp,)), dma((n_dp,)),
+            dma((2, n_dp)), dma((2, n_dp)), dma((2,)), dma((2,)),
+            dma((2, n_dp)), dma((2, n_dp)),
+        ],
+        compiler_params=pltpu.CompilerParams(
+            collective_id=0, has_side_effects=True, vmem_limit_bytes=32 * 1024 * 1024
+        ),
+    )(embeddings, assignment.reshape(1, rows), pair_list)
+    return best.reshape(rows)
+
+
+def general(embeddings, assignment, pair_list, capacity, n_dp, n_owner):
+    rows, width = embeddings.shape
     slots = capacity * n_dp
     values = embeddings.astype(jnp.float32)
     unit = (values * lax.rsqrt(jnp.sum(values * values, axis=1, keepdims=True) + 1e-06)).astype(
@@ -42,9 +273,7 @@
     partner = jnp.sum(jnp.where(picked, partners_mine[None, :], 0), axis=1)
     rows_p = lax.all_gather(mine, "owner", axis=0, tiled=True)
     ids_p = lax.all_gather(mine_ids, "owner", axis=0, tiled=True)
-    scores = lax.dot_general(
-        mine, rows_p, (((1,), (1,)), ((), ())), preferred_element_type=jnp.float32
-    )
+    scores = lax.dot_general(mine, rows_p, NT, preferred_element_type=jnp.float32)
     column = jnp.arange(ids_p.shape[0], dtype=jnp.int32)
     itself = here_owner * slots + jnp.arange(slots, dtype=jnp.int32)
     same = (
@@ -60,6 +289,15 @@
     return returned.reshape(slots)[position]
 
 
+def shards(embeddings, assignment, pair_list):
+    n_dp = lax.axis_size("dp")
+    n_owner = lax.axis_size("owner")
+    capacity = 2 * embeddings.shape[0] // n_dp
+    whole_tiles = n_dp == 8 and n_owner == 4 and capacity % 16 == 0
+    form = fused if whole_tiles else general
+    return form(embeddings, assignment, pair_list, capacity, n_dp, n_owner)
+
+
 def solution(mesh):
     placed = (P(("dp", "owner"), None), P(("dp", "owner")), P())
     return jax.shard_map(

time: 80.5 us -> 34.3 us (0.43)
  Pallas kernels: 0 us -> 31.4 us
  blocking collectives: 26.8 us -> 0 us
  waiting for transfers between devices: 15.6 us -> 0 us
  between operations: 13.5 us -> 0.01 us
  starting transfers between devices: 9.11 us -> 0 us
  other arithmetic: 6.08 us -> 0 us
  local copies, waits for them, and re-layouts: 6.24 us -> 2.8 us
  matrix products: 2.81 us -> 0 us
    pallas_call x0 -> x1, Pallas kernels: none -> 31.4 us  [fused(): pl.pallas_call(functools.partial(kernel, capacity, n_dp, n_owner), out_sh...]
    all_to_all x1 -> x0, blocking collectives: 21.7 us -> none  [shards(): lax.all_to_all(send_rows.reshape(n_dp, capacity, width), 'dp', split_axis...]
    all_to_all x2 -> x0, waiting for transfers between devices: 12.1 us -> none  [the longest x1 6.46 us: shards(): lax.all_to_all(best.reshape(n_dp, capacity), 'dp', split_axis=0, concat_a...]
    all_to_all x2 -> x0, starting transfers between devices: 9.1 us -> none  [the longest x1 5.52 us: shards(): lax.all_to_all(best.reshape(n_dp, capacity), 'dp', split_axis=0, concat_a...]
    all_gather x1 -> x0, blocking collectives: 5.06 us -> none  [shards(): ids_p = lax.all_gather(mine_ids, 'owner', axis=0, tiled=True)]
    all_gather x1 -> x0, waiting for transfers between devices: 3.44 us -> none  [shards(): rows_p = lax.all_gather(mine, 'owner', axis=0, tiled=True)]
    dot_general x1 -> x0, matrix products: 2.81 us -> none  [shards(): lax.dot_general(mine, rows_p, (((1,), (1,)), ((), ())), preferred_element...]
    unnamed x1 -> x7, local copies, waits for them, and re-layouts: 0.08 us -> 2.8 us
  transfers between devices with their start and end apart: 3 -> 0, of which waited for: 3 -> 0; matrix products, arithmetic and copies ran while one was open for 4% -> 0% of each run, Pallas kernels for 0% -> 0%
where the time goes in v1:
time: 34.3 us; the launch traced here: 34.2 us
  Pallas kernels  31.4 us (92%)
  local copies, waits for them, and re-layouts  2.8 us (8%)
    pallas_call x1, Pallas kernels, fused(): pl.pallas_call(functools.partial(kernel, capacity, n_dp, n_owner), out_sh...  31.4 us
    unnamed x7, local copies, waits for them, and re-layouts  2.8 us

profile of v1, /device:TPU:0, one launch (start us, length us, event | category | flops | bytes accessed | tf_op | source)
XLA Modules:
  0.0 34.2 jit_solution(18401441238876962069)
XLA Ops:
  0.0 0.0 copy-start.2
  0.0 0.7 %copy-done.2 = s32[128]{0:T(128)S(1)} copy-done((s32[128]{0:T(128)S(1)}, s32[128]{0:T(128)}, u32[]{:S(2)}) %copy-start.2) | copy-done | bytes 536
  0.7 0.0 copy-start
  0.7 0.9 %copy-done = bf16[128,1024]{1,0:T(8,128)(2,1)S(1)} copy-done((bf16[128,1024]{1,0:T(8,128)(2,1)S(1)}, bf16[128,1024]{1,0:T(8,128)(2,1)}, u32[]{:S(2)}) %copy-start) | copy-done | bytes 262168
  1.6 0.0 copy-start.1
  1.6 0.7 %copy-done.1 = s32[512]{0:T(512)S(1)} copy-done((s32[512]{0:T(512)S(1)}, s32[512]{0:T(512)}, u32[]{:S(2)}) %copy-start.1) | copy-done | bytes 2072
  2.3 31.4 %shard_map.37 = f32[1,128]{1,0:T(1,128)S(1)} custom-call(bf16[128,1024]{1,0:T(8,128)(2,1)S(1)} %copy-done, s32[1,128]{1,0:T(1,128)S(1)} %bitcast.2, s32[512]{0:T(512)S(1)} %copy-done.1), custom_call_target="tpu_custom_call" | custom-call | tf_op jit(solution)/shard_map/pallas_call | solution.py:217
  33.7 0.5 %copy.5 = f32[128]{0:T(128)} copy(f32[128]{0:T(128)S(1)} %bitcast.3) | data formatting | bytes 1024
Async XLA Ops:
  0.0 0.7 %copy-start.2 = (s32[128]{0:T(128)S(1)}, s32[128]{0:T(128)}, u32[]{:S(2)}) copy-start(s32[128]{0:T(128)} %param.4) | copy-start | bytes 1540
  0.7 0.9 %copy-start = (bf16[128,1024]{1,0:T(8,128)(2,1)S(1)}, bf16[128,1024]{1,0:T(8,128)(2,1)}, u32[]{:S(2)}) copy-start(bf16[128,1024]{1,0:T(8,128)(2,1)} %emb.1) | copy-start | bytes 786436
  1.6 0.7 %copy-start.1 = (s32[512]{0:T(512)S(1)}, s32[512]{0:T(512)}, u32[]{:S(2)}) copy-start(s32[512]{0:T(512)} %pairs.1) | copy-start | bytes 6148

commit v2 on v1

--- a/solution.py
+++ b/solution.py
@@ -26,19 +26,28 @@
     return z * 2 + y
 
 
-SEND_ORDER = (4, 5, 6, 7, 2, 3, 1)
-WAIT_ORDER = (1, 2, 3, 4, 6, 5, 7)
+NEAR = (1, 2, 3)
+CROSS = (4, 6, 5, 7)
+SEND_ORDER = (4, 6, 5, 7, 2, 3, 1)
 
 
 def kernel(
     cap, n_dp, n_owner,
-    emb, asg, pairs, out,
+    emb_hbm, asg_hbm, pairs_hbm, out,
+    emb, asg, pairs,
     send, own, sib, cpt,
-    code_send, code_got, codes, ret, res,
+    code_send, code_got, codes, columns, ret, res,
+    in_s,
     row_ss, row_rs, id_ss, id_rs, fw_ss, fw_rs, cd_ss, cd_rs, rt_ss, rt_rs,
 ):
     rows, width = emb.shape
     slots = cap * n_dp
+    loads = [
+        pltpu.make_async_copy(src, dst, in_s.at[i])
+        for i, (src, dst) in enumerate(((asg_hbm, asg), (emb_hbm, emb), (pairs_hbm, pairs)))
+    ]
+    for load in loads:
+        load.start()
     d = lax.axis_index("dp")
     o = lax.axis_index("owner")
     o_sib = o + 1 - 2 * (o % 2)
@@ -52,6 +61,7 @@
         pl.semaphore_signal(barrier, inc=1, device_id=(peers[k], o_sib), device_id_type=MESH)
     pl.semaphore_signal(barrier, inc=1, device_id=(d, o_cpt), device_id_type=MESH)
 
+    loads[0].wait()
     a = asg[...]
     t_row = lax.shift_right_logical(a, 6)
     code_row = ((a & 63) + 1).astype(jnp.float32)
@@ -73,6 +83,7 @@
     for t in range(n_dp):
         code_send[t] = slot_codes[t : t + 1, :]
 
+    loads[1].wait()
     values = emb[...].astype(jnp.float32)
     unit = (values * lax.rsqrt(jnp.sum(values * values, axis=1, keepdims=True) + 1e-06)).astype(
         jnp.bfloat16
@@ -120,25 +131,27 @@
             recv_sem=rt_rs.at[which, k], device_id=(s, (o, o_sib)[which]), device_id_type=MESH,
         )
 
+    for k in CROSS[:2]:
+        block_copy(k).start()
+    forward(0, 1).start()
+    for k in NEAR:
+        block_copy(k).start()
     for k in SEND_ORDER:
         code_copy(k).start()
-    for k in SEND_ORDER:
-        block_copy(k).start()
-    forward(0, 1).start()
     forward(0, 0).start()
-    for k in WAIT_ORDER:
+    for i, k in enumerate(NEAR):
+        block_copy(k).wait_recv()
+        forward(k, 1).start()
+        forward(k, 0).start()
+        if i < 2:
+            block_copy(CROSS[2 + i]).start()
+    for k in NEAR + CROSS:
         code_copy(k).wait_recv()
     codes[0] = jnp.sum(code_got[...], axis=0)
     codes_copy(0).start()
     codes_copy(1).start()
-    for k in WAIT_ORDER:
-        block_copy(k).wait_recv()
-        forward(k, 1).start()
-        forward(k, 0).start()
-
-    codes_copy(0).wait_recv()
-    codes_copy(1).wait_recv()
-    g_own, g_sib, g_cpt = codes[0], codes[1], codes[2]
+    loads[2].wait()
+    g_own = codes[0]
 
     def partner(g, owner):
         found = jnp.full(g.shape, -1, jnp.int32)
@@ -147,19 +160,32 @@
             found = jnp.where(g == (owner * CPD + c + 1).astype(jnp.float32), other, found)
         return found.astype(jnp.float32)
 
-    p_own, p_sib = partner(g_own, o), partner(g_sib, o_sib)
-
     def column(g):
         return jnp.transpose(jnp.broadcast_to(g, (128, slots)))
 
+    p_own = partner(g_own, o)
+    columns[0] = column(g_own)
+    block_copy(CROSS[0]).wait_recv()
+    forward(CROSS[0], 1).start()
+    forward(CROSS[0], 0).start()
+    codes_copy(0).wait_recv()
+    codes_copy(1).wait_recv()
+    p_sib = partner(codes[1], o_sib)
+    columns[1] = column(codes[1])
+    columns[2] = column(codes[2])
+    for k in CROSS[1:]:
+        block_copy(k).wait_recv()
+        forward(k, 1).start()
+        forward(k, 0).start()
+
     def table(ref):
         return ref[...].reshape(slots, width)
 
     def scores(keys, queries):
         return lax.dot_general(keys, queries, NT, preferred_element_type=jnp.float32)
 
-    def wide(column_128):
-        return jnp.concatenate([column_128] * (slots // 128), axis=1)
+    def wide(which):
+        return jnp.concatenate([columns[which]] * (slots // 128), axis=1)
 
     def masked_max(s, mask):
         return jnp.max(jnp.where(mask, s, -1.0), axis=0, keepdims=True)
@@ -167,15 +193,15 @@
     rows_own = table(own)
     key = lax.broadcasted_iota(jnp.int32, (slots, slots), 0)
     query = lax.broadcasted_iota(jnp.int32, (slots, slots), 1)
-    best = masked_max(scores(rows_own, rows_own), (wide(column(g_own)) == g_own) & (key != query))
+    best = masked_max(scores(rows_own, rows_own), (wide(0) == g_own) & (key != query))
     for k in range(n_dp):
         forward(k, 0).wait_recv()
     rows_sib = table(sib)
-    best = jnp.maximum(best, masked_max(scores(rows_sib, rows_own), wide(column(g_sib)) == p_own))
+    best = jnp.maximum(best, masked_max(scores(rows_sib, rows_own), wide(1) == p_own))
     for k in range(n_dp):
         forward(k, 1).wait_recv()
     rows_cpt = table(cpt)
-    k_cpt = wide(column(g_cpt))
+    k_cpt = wide(2)
     res[1] = masked_max(scores(rows_cpt, rows_sib), k_cpt == p_sib)
     for k in (4, 5, 6, 7, 2, 3, 1, 0):
         back(k, 1).start()
@@ -194,7 +220,7 @@
         got, lane_hot, (((1,), (0,)), ((), ())),
         preferred_element_type=jnp.float32, precision=lax.Precision.HIGHEST,
     )
-    out[...] = jnp.maximum(jnp.sum(t_hot * picked, axis=0, keepdims=True), -1.0)
+    out[...] = jnp.sum(t_hot * picked, axis=0, keepdims=True)
 
     for k in range(n_dp):
         if k:
@@ -217,27 +243,28 @@
     best = pl.pallas_call(
         functools.partial(kernel, capacity, n_dp, n_owner),
         out_shape=jax.ShapeDtypeStruct((1, rows), jnp.float32),
-        in_specs=[
-            pl.BlockSpec(memory_space=pltpu.VMEM),
-            pl.BlockSpec(memory_space=pltpu.VMEM),
-            pl.BlockSpec(memory_space=pltpu.SMEM),
-        ],
+        in_specs=[pl.BlockSpec(memory_space=pl.ANY)] * 3,
         out_specs=pl.BlockSpec(memory_space=pltpu.VMEM),
         scratch_shapes=[
+            pltpu.VMEM((rows, width), jnp.bfloat16),
+            pltpu.VMEM((1, rows), jnp.int32),
+            pltpu.SMEM(pair_list.shape, jnp.int32),
             block, block, block, block,
             line, line,
             pltpu.VMEM((3, 1, slots), jnp.float32),
+            pltpu.VMEM((3, slots, 128), jnp.float32),
             pltpu.VMEM((2, n_dp, 1, slots), jnp.float32),
             pltpu.VMEM((2, 1, slots), jnp.float32),
+            dma((3,)),
             dma((n_dp,)), dma((n_dp,)), dma((n_dp,)), dma((n_dp,)),
             dma((2, n_dp)), dma((2, n_dp)), dma((2,)), dma((2,)),
             dma((2, n_dp)), dma((2, n_dp)),
         ],
         compiler_params=pltpu.CompilerParams(
-            collective_id=0, has_side_effects=True, vmem_limit_bytes=32 * 1024 * 1024
+            collective_id=0, has_side_effects=True, vmem_limit_bytes=60 * 1024 * 1024
         ),
     )(embeddings, assignment.reshape(1, rows), pair_list)
-    return best.reshape(rows)
+    return jnp.maximum(best.reshape(rows), -1.0)
 
 
 def general(embeddings, assignment, pair_list, capacity, n_dp, n_owner):

time: 34.3 us -> 31.4 us (0.915)
  local copies, waits for them, and re-layouts: 2.8 us -> 0 us
  Pallas kernels: 31.4 us -> 30 us
  other arithmetic: 0 us -> 1.19 us
    unnamed x7 -> x0, local copies, waits for them, and re-layouts: 2.8 us -> none
    pallas_call x1, Pallas kernels: 31.4 us -> 30 us  [fused(): pl.pallas_call(functools.partial(kernel, capacity, n_dp, n_owner), out_sh...]
    max x0 -> x1, other arithmetic: none -> 1.19 us  [fused(): return jnp.maximum(best.reshape(rows), -1.0)]
where the time goes in v2:
time: 31.4 us; the launch traced here: 31.2 us
  Pallas kernels  30 us (96%)
  other arithmetic  1.19 us (4%)
    pallas_call x1, Pallas kernels, fused(): pl.pallas_call(functools.partial(kernel, capacity, n_dp, n_owner), out_sh...  30 us
    max x1, other arithmetic, fused(): return jnp.maximum(best.reshape(rows), -1.0)  1.19 us

profile of v2, /device:TPU:0, one launch (start us, length us, event | category | flops | bytes accessed | tf_op | source)
XLA Modules:
  0.0 31.2 jit_solution(2378334736777321515)
XLA Ops:
  0.0 30.0 %shard_map.37 = f32[1,128]{1,0:T(1,128)} custom-call(bf16[128,1024]{1,0:T(8,128)(2,1)} %emb_hbm.1, s32[1,128]{1,0:T(1,128)} %bitcast.3, s32[512]{0:T(512)} %pairs_hbm.1), custom_call_target="tpu_custom_call" | custom-call | tf_op jit(solution)/shard_map/pallas_call | solution.py:243
  30.1 1.2 %maximum_bitcast_fusion = f32[128]{0:T(128)} fusion(f32[1,128]{1,0:T(1,128)} %shard_map.37), kind=kLoop, calls=%fused_computation | loop fusion | flops 128 | bytes 1024 | tf_op jit(solution)/shard_map/max | solution.py:267

commit v3 on v2

--- a/solution.py
+++ b/solution.py
@@ -28,6 +28,8 @@
 
 NEAR = (1, 2, 3)
 CROSS = (4, 6, 5, 7)
+PIECES = tuple((k, h) for k in CROSS for h in range(2))
+AHEAD = 3
 SEND_ORDER = (4, 6, 5, 7, 2, 3, 1)
 
 
@@ -88,19 +90,30 @@
     unit = (values * lax.rsqrt(jnp.sum(values * values, axis=1, keepdims=True) + 1e-06)).astype(
         jnp.bfloat16
     )
-    place = (slot_iota == t_row * cap + rank).astype(jnp.float32).astype(jnp.bfloat16)
-    packed = jnp.dot(place, unit, preferred_element_type=jnp.float32).astype(jnp.bfloat16)
-    for t in range(n_dp):
-        send[t] = packed[t * cap : (t + 1) * cap, :]
-    own[d] = send[d]
+    position = t_row * cap + rank
+    half = n_dp // 2
+    near_base = (d // half) * half
+    cross_base = half - near_base
+    group_iota = lax.broadcasted_iota(jnp.int32, (half * cap, rows), 0)
+
+    def pack(base):
+        place = (group_iota + base * cap == position).astype(jnp.float32).astype(jnp.bfloat16)
+        packed = jnp.dot(place, unit, preferred_element_type=jnp.float32).astype(jnp.bfloat16)
+        send[pl.ds(base, half)] = packed.reshape(half, cap, width)
+
+    pack(cross_base)
     code_got[d] = code_send[d]
 
     pl.semaphore_wait(barrier, 2 * n_dp)
 
-    def block_copy(k):
+    def part(h):
+        return pl.ds(0, cap) if h is None else pl.ds(h * (cap // 2), cap // 2)
+
+    def block_copy(k, h=None):
         p = peers[k]
         return pltpu.make_async_remote_copy(
-            src_ref=send.at[p], dst_ref=own.at[d], send_sem=row_ss.at[k], recv_sem=row_rs.at[k],
+            src_ref=send.at[p, part(h)], dst_ref=own.at[d, part(h)],
+            send_sem=row_ss.at[k, h or 0], recv_sem=row_rs.at[k, h or 0],
             device_id=(p, o), device_id_type=MESH,
         )
 
@@ -111,11 +124,12 @@
             recv_sem=id_rs.at[k], device_id=(p, o), device_id_type=MESH,
         )
 
-    def forward(k, which):
+    def forward(k, which, h=None):
         s = peers[k]
         return pltpu.make_async_remote_copy(
-            src_ref=own.at[s], dst_ref=(sib, cpt)[which].at[s], send_sem=fw_ss.at[which, k],
-            recv_sem=fw_rs.at[which, k], device_id=(d, (o_sib, o_cpt)[which]), device_id_type=MESH,
+            src_ref=own.at[s, part(h)], dst_ref=(sib, cpt)[which].at[s, part(h)],
+            send_sem=fw_ss.at[which, k, h or 0], recv_sem=fw_rs.at[which, k, h or 0],
+            device_id=(d, (o_sib, o_cpt)[which]), device_id_type=MESH,
         )
 
     def codes_copy(which):
@@ -131,20 +145,20 @@
             recv_sem=rt_rs.at[which, k], device_id=(s, (o, o_sib)[which]), device_id_type=MESH,
         )
 
-    for k in CROSS[:2]:
-        block_copy(k).start()
-    forward(0, 1).start()
+    for k in SEND_ORDER:
+        code_copy(k).start()
+    for k, h in PIECES[:AHEAD]:
+        block_copy(k, h).start()
+    pack(near_base)
     for k in NEAR:
         block_copy(k).start()
-    for k in SEND_ORDER:
-        code_copy(k).start()
+    own[d] = send[d]
+    forward(0, 1).start()
     forward(0, 0).start()
-    for i, k in enumerate(NEAR):
+    for k in NEAR:
         block_copy(k).wait_recv()
         forward(k, 1).start()
         forward(k, 0).start()
-        if i < 2:
-            block_copy(CROSS[2 + i]).start()
     for k in NEAR + CROSS:
         code_copy(k).wait_recv()
     codes[0] = jnp.sum(code_got[...], axis=0)
@@ -153,6 +167,16 @@
     loads[2].wait()
     g_own = codes[0]
 
+    def pieces(first, last):
+        for i in range(first, last):
+            k, h = PIECES[i]
+            block_copy(k, h).wait_recv()
+            forward(k, 1, h).start()
+            if h:
+                forward(k, 0).start()
+            if i + AHEAD < len(PIECES):
+                block_copy(*PIECES[i + AHEAD]).start()
+
     def partner(g, owner):
         found = jnp.full(g.shape, -1, jnp.int32)
         for c in range(CPD):
@@ -165,18 +189,13 @@
 
     p_own = partner(g_own, o)
     columns[0] = column(g_own)
-    block_copy(CROSS[0]).wait_recv()
-    forward(CROSS[0], 1).start()
-    forward(CROSS[0], 0).start()
+    pieces(0, 2)
     codes_copy(0).wait_recv()
     codes_copy(1).wait_recv()
     p_sib = partner(codes[1], o_sib)
     columns[1] = column(codes[1])
     columns[2] = column(codes[2])
-    for k in CROSS[1:]:
-        block_copy(k).wait_recv()
-        forward(k, 1).start()
-        forward(k, 0).start()
+    pieces(2, len(PIECES))
 
     def table(ref):
         return ref[...].reshape(slots, width)
@@ -184,8 +203,8 @@
     def scores(keys, queries):
         return lax.dot_general(keys, queries, NT, preferred_element_type=jnp.float32)
 
-    def wide(which):
-        return jnp.concatenate([columns[which]] * (slots // 128), axis=1)
+    def wide(column_128):
+        return jnp.concatenate([column_128] * (slots // 128), axis=1)
 
     def masked_max(s, mask):
         return jnp.max(jnp.where(mask, s, -1.0), axis=0, keepdims=True)
@@ -193,19 +212,29 @@
     rows_own = table(own)
     key = lax.broadcasted_iota(jnp.int32, (slots, slots), 0)
     query = lax.broadcasted_iota(jnp.int32, (slots, slots), 1)
-    best = masked_max(scores(rows_own, rows_own), (wide(0) == g_own) & (key != query))
+    best = masked_max(scores(rows_own, rows_own), (wide(columns[0]) == g_own) & (key != query))
     for k in range(n_dp):
         forward(k, 0).wait_recv()
     rows_sib = table(sib)
-    best = jnp.maximum(best, masked_max(scores(rows_sib, rows_own), wide(1) == p_own))
-    for k in range(n_dp):
+    best = jnp.maximum(best, masked_max(scores(rows_sib, rows_own), wide(columns[1]) == p_own))
+    best_sib = jnp.full((1, slots), -1.0, jnp.float32)
+
+    def neighbour_keys(base):
+        keys = cpt[pl.ds(base, half)].reshape(half * cap, width)
+        return keys, wide(columns[2, pl.ds(pl.multiple_of(base * cap, half * cap), half * cap)])
+
+    for k in (0,) + NEAR:
         forward(k, 1).wait_recv()
-    rows_cpt = table(cpt)
-    k_cpt = wide(2)
-    res[1] = masked_max(scores(rows_cpt, rows_sib), k_cpt == p_sib)
+    keys, key_codes = neighbour_keys(near_base)
+    best_sib = jnp.maximum(best_sib, masked_max(scores(keys, rows_sib), key_codes == p_sib))
+    best = jnp.maximum(best, masked_max(scores(keys, rows_own), key_codes == p_own))
+    for k, h in PIECES:
+        forward(k, 1, h).wait_recv()
+    keys, key_codes = neighbour_keys(cross_base)
+    res[1] = jnp.maximum(best_sib, masked_max(scores(keys, rows_sib), key_codes == p_sib))
     for k in (4, 5, 6, 7, 2, 3, 1, 0):
         back(k, 1).start()
-    best = jnp.maximum(best, masked_max(scores(rows_cpt, rows_own), k_cpt == p_own))
+    best = jnp.maximum(best, masked_max(scores(keys, rows_own), key_codes == p_own))
     res[0] = best
     for k in SEND_ORDER:
         back(k, 0).start()
@@ -220,16 +249,21 @@
         got, lane_hot, (((1,), (0,)), ((), ())),
         preferred_element_type=jnp.float32, precision=lax.Precision.HIGHEST,
     )
-    out[...] = jnp.sum(t_hot * picked, axis=0, keepdims=True)
-
-    for k in range(n_dp):
+    out[...] = jnp.maximum(jnp.sum(t_hot * picked, axis=0, keepdims=True), -1.0)
+
+    for k in (0,) + NEAR + CROSS:
         if k:
-            block_copy(k).wait_send()
             code_copy(k).wait_send()
             back(k, 0).wait_send()
+        if k in NEAR:
+            block_copy(k).wait_send()
+        if k not in CROSS:
+            forward(k, 1).wait_send()
         back(k, 1).wait_send()
         forward(k, 0).wait_send()
-        forward(k, 1).wait_send()
+    for k, h in PIECES:
+        block_copy(k, h).wait_send()
+        forward(k, 1, h).wait_send()
     codes_copy(0).wait_send()
     codes_copy(1).wait_send()
 
@@ -240,6 +274,10 @@
     block = pltpu.VMEM((n_dp, capacity, width), jnp.bfloat16)
     line = pltpu.VMEM((n_dp, 1, slots), jnp.float32)
     dma = pltpu.SemaphoreType.DMA
+    operands = [
+        pltpu.with_memory_space_constraint(x, pltpu.HBM)
+        for x in (embeddings, assignment.reshape(1, rows), pair_list)
+    ]
     best = pl.pallas_call(
         functools.partial(kernel, capacity, n_dp, n_owner),
         out_shape=jax.ShapeDtypeStruct((1, rows), jnp.float32),
@@ -256,15 +294,15 @@
             pltpu.VMEM((2, n_dp, 1, slots), jnp.float32),
             pltpu.VMEM((2, 1, slots), jnp.float32),
             dma((3,)),
-            dma((n_dp,)), dma((n_dp,)), dma((n_dp,)), dma((n_dp,)),
-            dma((2, n_dp)), dma((2, n_dp)), dma((2,)), dma((2,)),
+            dma((n_dp, 2)), dma((n_dp, 2)), dma((n_dp,)), dma((n_dp,)),
+            dma((2, n_dp, 2)), dma((2, n_dp, 2)), dma((2,)), dma((2,)),
             dma((2, n_dp)), dma((2, n_dp)),
         ],
         compiler_params=pltpu.CompilerParams(
-            collective_id=0, has_side_effects=True, vmem_limit_bytes=60 * 1024 * 1024
+            collective_id=0, has_side_effects=True, vmem_limit_bytes=32 * 1024 * 1024
         ),
-    )(embeddings, assignment.reshape(1, rows), pair_list)
-    return jnp.maximum(best.reshape(rows), -1.0)
+    )(*operands)
+    return best.reshape(rows)
 
 
 def general(embeddings, assignment, pair_list, capacity, n_dp, n_owner):

time: 31.4 us -> 33.3 us (1.061)
  Pallas kernels: 30 us -> 32.6 us
  other arithmetic: 1.19 us -> 0 us
  local copies, waits for them, and re-layouts: 0 us -> 0.51 us
    pallas_call x1, Pallas kernels: 30 us -> 32.6 us  [fused(): pl.pallas_call(functools.partial(kernel, capacity, n_dp, n_owner), out_sh...]
    max x1 -> x0, other arithmetic: 1.19 us -> none  [fused(): return jnp.maximum(best.reshape(rows), -1.0)]
    unnamed x0 -> x1, local copies, waits for them, and re-layouts: none -> 0.51 us
where the time goes in v3:
time: 33.3 us; the launch traced here: 33.1 us
  Pallas kernels  32.6 us (98%)
  local copies, waits for them, and re-layouts  0.51 us (2%)
    pallas_call x1, Pallas kernels, fused(): pl.pallas_call(functools.partial(kernel, capacity, n_dp, n_owner), out_sh...  32.6 us

profile of v3, /device:TPU:0, one launch (start us, length us, event | category | flops | bytes accessed | tf_op | source)
XLA Modules:
  0.0 33.1 jit_solution(12323173734856046350)
XLA Ops:
  0.0 32.6 %shard_map.37 = f32[1,128]{1,0:T(1,128)S(1)} custom-call(bf16[128,1024]{1,0:T(8,128)(2,1)} %emb_hbm.1, s32[1,128]{1,0:T(1,128)} %bitcast.3, s32[512]{0:T(512)} %pairs_hbm.1), custom_call_target="tpu_custom_call" | custom-call | tf_op jit(solution)/shard_map/pallas_call | solution.py:281
  32.6 0.5 %copy.5 = f32[128]{0:T(128)} copy(f32[128]{0:T(128)S(1)} %bitcast.2) | data formatting | bytes 1024

commit v4 on v3

--- a/solution.py
+++ b/solution.py
@@ -28,8 +28,8 @@
 
 NEAR = (1, 2, 3)
 CROSS = (4, 6, 5, 7)
-PIECES = tuple((k, h) for k in CROSS for h in range(2))
-AHEAD = 3
+PIECES = tuple((k, None) for k in CROSS)
+AHEAD = 4
 SEND_ORDER = (4, 6, 5, 7, 2, 3, 1)
 
 
@@ -172,7 +172,7 @@
             k, h = PIECES[i]
             block_copy(k, h).wait_recv()
             forward(k, 1, h).start()
-            if h:
+            if h != 0:
                 forward(k, 0).start()
             if i + AHEAD < len(PIECES):
                 block_copy(*PIECES[i + AHEAD]).start()
@@ -189,13 +189,13 @@
 
     p_own = partner(g_own, o)
     columns[0] = column(g_own)
-    pieces(0, 2)
+    pieces(0, 1)
     codes_copy(0).wait_recv()
     codes_copy(1).wait_recv()
     p_sib = partner(codes[1], o_sib)
     columns[1] = column(codes[1])
     columns[2] = column(codes[2])
-    pieces(2, len(PIECES))
+    pieces(1, len(PIECES))
 
     def table(ref):
         return ref[...].reshape(slots, width)

time: 33.3 us -> 31.9 us (0.958)
  Pallas kernels: 32.6 us -> 31.2 us
    pallas_call x1, Pallas kernels: 32.6 us -> 31.2 us  [fused(): pl.pallas_call(functools.partial(kernel, capacity, n_dp, n_owner), out_sh...]
where the time goes in v4:
time: 31.9 us; the launch traced here: 31.8 us
  Pallas kernels  31.2 us (98%)
  local copies, waits for them, and re-layouts  0.51 us (2%)
    pallas_call x1, Pallas kernels, fused(): pl.pallas_call(functools.partial(kernel, capacity, n_dp, n_owner), out_sh...  31.2 us

profile of v4, /device:TPU:0, one launch (start us, length us, event | category | flops | bytes accessed | tf_op | source)
XLA Modules:
  0.0 31.8 jit_solution(18313256451874462319)
XLA Ops:
  0.0 31.2 %shard_map.37 = f32[1,128]{1,0:T(1,128)S(1)} custom-call(bf16[128,1024]{1,0:T(8,128)(2,1)} %emb_hbm.1, s32[1,128]{1,0:T(1,128)} %bitcast.3, s32[512]{0:T(512)} %pairs_hbm.1), custom_call_target="tpu_custom_call" | custom-call | tf_op jit(solution)/shard_map/pallas_call | solution.py:281
  31.2 0.5 %copy.5 = f32[128]{0:T(128)} copy(f32[128]{0:T(128)S(1)} %bitcast.2) | data formatting | bytes 1024

commit v5 on v4

--- a/solution.py
+++ b/solution.py
@@ -101,7 +101,8 @@
         packed = jnp.dot(place, unit, preferred_element_type=jnp.float32).astype(jnp.bfloat16)
         send[pl.ds(base, half)] = packed.reshape(half, cap, width)
 
-    pack(cross_base)
+    pack(near_base)
+    own[d] = send[d]
     code_got[d] = code_send[d]
 
     pl.semaphore_wait(barrier, 2 * n_dp)
@@ -145,19 +146,20 @@
             recv_sem=rt_rs.at[which, k], device_id=(s, (o, o_sib)[which]), device_id_type=MESH,
         )
 
+    for k in NEAR:
+        block_copy(k).start()
+    forward(0, 1).start()
     for k in SEND_ORDER:
         code_copy(k).start()
-    for k, h in PIECES[:AHEAD]:
+    pack(cross_base)
+    for k, h in PIECES[:2]:
         block_copy(k, h).start()
-    pack(near_base)
-    for k in NEAR:
-        block_copy(k).start()
-    own[d] = send[d]
-    forward(0, 1).start()
-    forward(0, 0).start()
     for k in NEAR:
         block_copy(k).wait_recv()
         forward(k, 1).start()
+        if k > 1:
+            block_copy(*PIECES[k]).start()
+    for k in (0,) + NEAR:
         forward(k, 0).start()
     for k in NEAR + CROSS:
         code_copy(k).wait_recv()

time: 31.9 us -> 30.7 us (0.962)
  Pallas kernels: 31.2 us -> 30 us
    pallas_call x1, Pallas kernels: 31.2 us -> 30 us  [fused(): pl.pallas_call(functools.partial(kernel, capacity, n_dp, n_owner), out_sh...]
where the time goes in v5:
time: 30.7 us; the launch traced here: 30.6 us
  Pallas kernels  30 us (98%)
  local copies, waits for them, and re-layouts  0.51 us (2%)
    pallas_call x1, Pallas kernels, fused(): pl.pallas_call(functools.partial(kernel, capacity, n_dp, n_owner), out_sh...  30 us

profile of v5, /device:TPU:0, one launch (start us, length us, event | category | flops | bytes accessed | tf_op | source)
XLA Modules:
  0.0 30.6 jit_solution(5315632003321737068)
XLA Ops:
  0.0 30.0 %shard_map.37 = f32[1,128]{1,0:T(1,128)S(1)} custom-call(bf16[128,1024]{1,0:T(8,128)(2,1)} %emb_hbm.1, s32[1,128]{1,0:T(1,128)} %bitcast.3, s32[512]{0:T(512)} %pairs_hbm.1), custom_call_target="tpu_custom_call" | custom-call | tf_op jit(solution)/shard_map/pallas_call | solution.py:283
  30.0 0.5 %copy.5 = f32[128]{0:T(128)} copy(f32[128]{0:T(128)S(1)} %bitcast.2) | data formatting | bytes 1024

commit v6 on v5

--- a/solution.py
+++ b/solution.py
@@ -28,8 +28,6 @@
 
 NEAR = (1, 2, 3)
 CROSS = (4, 6, 5, 7)
-PIECES = tuple((k, None) for k in CROSS)
-AHEAD = 4
 SEND_ORDER = (4, 6, 5, 7, 2, 3, 1)
 
 
@@ -102,19 +100,17 @@
         send[pl.ds(base, half)] = packed.reshape(half, cap, width)
 
     pack(near_base)
+    pack(cross_base)
     own[d] = send[d]
     code_got[d] = code_send[d]
 
     pl.semaphore_wait(barrier, 2 * n_dp)
 
-    def part(h):
-        return pl.ds(0, cap) if h is None else pl.ds(h * (cap // 2), cap // 2)
-
-    def block_copy(k, h=None):
+    def block_copy(k):
         p = peers[k]
         return pltpu.make_async_remote_copy(
-            src_ref=send.at[p, part(h)], dst_ref=own.at[d, part(h)],
-            send_sem=row_ss.at[k, h or 0], recv_sem=row_rs.at[k, h or 0],
+            src_ref=send.at[p], dst_ref=own.at[d],
+            send_sem=row_ss.at[k], recv_sem=row_rs.at[k],
             device_id=(p, o), device_id_type=MESH,
         )
 
@@ -125,11 +121,11 @@
             recv_sem=id_rs.at[k], device_id=(p, o), device_id_type=MESH,
         )
 
-    def forward(k, which, h=None):
+    def forward(k, which):
         s = peers[k]
         return pltpu.make_async_remote_copy(
-            src_ref=own.at[s, part(h)], dst_ref=(sib, cpt)[which].at[s, part(h)],
-            send_sem=fw_ss.at[which, k, h or 0], recv_sem=fw_rs.at[which, k, h or 0],
+            src_ref=own.at[s], dst_ref=(sib, cpt)[which].at[s],
+            send_sem=fw_ss.at[which, k], recv_sem=fw_rs.at[which, k],
             device_id=(d, (o_sib, o_cpt)[which]), device_id_type=MESH,
         )
 
@@ -146,21 +142,36 @@
             recv_sem=rt_rs.at[which, k], device_id=(s, (o, o_sib)[which]), device_id_type=MESH,
         )
 
-    for k in NEAR:
-        block_copy(k).start()
-    forward(0, 1).start()
-    for k in SEND_ORDER:
-        code_copy(k).start()
-    pack(cross_base)
-    for k, h in PIECES[:2]:
-        block_copy(k, h).start()
-    for k in NEAR:
-        block_copy(k).wait_recv()
-        forward(k, 1).start()
-        if k > 1:
-            block_copy(*PIECES[k]).start()
-    for k in (0,) + NEAR:
-        forward(k, 0).start()
+    def pass_on(ks):
+        for k in ks:
+            block_copy(k).wait_recv()
+            forward(k, 1).start()
+
+    def send_codes():
+        for k in SEND_ORDER:
+            code_copy(k).start()
+
+    first_core = o % 2 == 0
+    second_core = o % 2 == 1
+
+    @pl.when(first_core)
+    def _():
+        send_codes()
+        for k in CROSS + NEAR:
+            block_copy(k).start()
+        forward(0, 1).start()
+        pass_on(CROSS[:2])
+
+    @pl.when(second_core)
+    def _():
+        for k in NEAR:
+            block_copy(k).start()
+        forward(0, 1).start()
+        send_codes()
+        pass_on(NEAR)
+        for k in CROSS:
+            block_copy(k).start()
+
     for k in NEAR + CROSS:
         code_copy(k).wait_recv()
     codes[0] = jnp.sum(code_got[...], axis=0)
@@ -169,16 +180,6 @@
     loads[2].wait()
     g_own = codes[0]
 
-    def pieces(first, last):
-        for i in range(first, last):
-            k, h = PIECES[i]
-            block_copy(k, h).wait_recv()
-            forward(k, 1, h).start()
-            if h != 0:
-                forward(k, 0).start()
-            if i + AHEAD < len(PIECES):
-                block_copy(*PIECES[i + AHEAD]).start()
-
     def partner(g, owner):
         found = jnp.full(g.shape, -1, jnp.int32)
         for c in range(CPD):
@@ -191,13 +192,26 @@
 
     p_own = partner(g_own, o)
     columns[0] = column(g_own)
-    pieces(0, 1)
+
+    @pl.when(first_core)
+    def _():
+        pass_on(CROSS[2:] + NEAR)
+        for k in CROSS + (0,) + NEAR:
+            forward(k, 0).start()
+
+    @pl.when(second_core)
+    def _():
+        for k in (0,) + NEAR:
+            forward(k, 0).start()
+        for k in CROSS:
+            pass_on((k,))
+            forward(k, 0).start()
+
     codes_copy(0).wait_recv()
     codes_copy(1).wait_recv()
     p_sib = partner(codes[1], o_sib)
     columns[1] = column(codes[1])
     columns[2] = column(codes[2])
-    pieces(1, len(PIECES))
 
     def table(ref):
         return ref[...].reshape(slots, width)
@@ -225,14 +239,19 @@
         keys = cpt[pl.ds(base, half)].reshape(half * cap, width)
         return keys, wide(columns[2, pl.ds(pl.multiple_of(base * cap, half * cap), half * cap)])
 
-    for k in (0,) + NEAR:
-        forward(k, 1).wait_recv()
-    keys, key_codes = neighbour_keys(near_base)
+    def arrived(ks):
+        for k in ks:
+            forward(k, 1).wait_recv()
+
+    pl.when(first_core)(lambda: arrived(CROSS))
+    pl.when(second_core)(lambda: arrived((0,) + NEAR))
+    early_base = (1 - o % 2) * cross_base + (o % 2) * near_base
+    keys, key_codes = neighbour_keys(early_base)
     best_sib = jnp.maximum(best_sib, masked_max(scores(keys, rows_sib), key_codes == p_sib))
     best = jnp.maximum(best, masked_max(scores(keys, rows_own), key_codes == p_own))
-    for k, h in PIECES:
-        forward(k, 1, h).wait_recv()
-    keys, key_codes = neighbour_keys(cross_base)
+    pl.when(first_core)(lambda: arrived((0,) + NEAR))
+    pl.when(second_core)(lambda: arrived(CROSS))
+    keys, key_codes = neighbour_keys(half - early_base)
     res[1] = jnp.maximum(best_sib, masked_max(scores(keys, rows_sib), key_codes == p_sib))
     for k in (4, 5, 6, 7, 2, 3, 1, 0):
         back(k, 1).start()
@@ -257,15 +276,10 @@
         if k:
             code_copy(k).wait_send()
             back(k, 0).wait_send()
-        if k in NEAR:
             block_copy(k).wait_send()
-        if k not in CROSS:
-            forward(k, 1).wait_send()
+        forward(k, 1).wait_send()
         back(k, 1).wait_send()
         forward(k, 0).wait_send()
-    for k, h in PIECES:
-        block_copy(k, h).wait_send()
-        forward(k, 1, h).wait_send()
     codes_copy(0).wait_send()
     codes_copy(1).wait_send()
 
@@ -296,8 +310,8 @@
             pltpu.VMEM((2, n_dp, 1, slots), jnp.float32),
             pltpu.VMEM((2, 1, slots), jnp.float32),
             dma((3,)),
-            dma((n_dp, 2)), dma((n_dp, 2)), dma((n_dp,)), dma((n_dp,)),
-            dma((2, n_dp, 2)), dma((2, n_dp, 2)), dma((2,)), dma((2,)),
+            dma((n_dp,)), dma((n_dp,)), dma((n_dp,)), dma((n_dp,)),
+            dma((2, n_dp)), dma((2, n_dp)), dma((2,)), dma((2,)),
             dma((2, n_dp)), dma((2, n_dp)),
         ],
         compiler_params=pltpu.CompilerParams(

time: 30.7 us -> 30.5 us (level)
  no operation moved by 1% of the time
where the time goes in v6:
time: 30.5 us; the launch traced here: 30.3 us
  Pallas kernels  29.8 us (98%)
  local copies, waits for them, and re-layouts  0.51 us (2%)
    pallas_call x1, Pallas kernels, fused(): pl.pallas_call(functools.partial(kernel, capacity, n_dp, n_owner), out_sh...  29.8 us

profile of v6, /device:TPU:0, one launch (start us, length us, event | category | flops | bytes accessed | tf_op | source)
XLA Modules:
  0.0 30.3 jit_solution(17648064148171394474)
XLA Ops:
  0.0 29.8 %shard_map.37 = f32[1,128]{1,0:T(1,128)S(1)} custom-call(bf16[128,1024]{1,0:T(8,128)(2,1)} %emb_hbm.1, s32[1,128]{1,0:T(1,128)} %bitcast.3, s32[512]{0:T(512)} %pairs_hbm.1), custom_call_target="tpu_custom_call" | custom-call | tf_op jit(solution)/shard_map/pallas_call | solution.py:297
  29.8 0.5 %copy.5 = f32[128]{0:T(128)} copy(f32[128]{0:T(128)S(1)} %bitcast.2) | data formatting | bytes 1024

commit v7 on v5

--- a/solution.py
+++ b/solution.py
@@ -29,7 +29,7 @@
 NEAR = (1, 2, 3)
 CROSS = (4, 6, 5, 7)
 PIECES = tuple((k, None) for k in CROSS)
-AHEAD = 4
+AHEAD = 3
 SEND_ORDER = (4, 6, 5, 7, 2, 3, 1)
 
 
@@ -157,8 +157,8 @@
     for k in NEAR:
         block_copy(k).wait_recv()
         forward(k, 1).start()
-        if k > 1:
-            block_copy(*PIECES[k]).start()
+        if k == 2:
+            block_copy(*PIECES[2]).start()
     for k in (0,) + NEAR:
         forward(k, 0).start()
     for k in NEAR + CROSS:

time: 30.7 us -> 30.7 us (level)
  no operation moved by 1% of the time
where the time goes in v7:
time: 30.7 us; the launch traced here: 30.6 us
  Pallas kernels  30 us (98%)
  local copies, waits for them, and re-layouts  0.51 us (2%)
    pallas_call x1, Pallas kernels, fused(): pl.pallas_call(functools.partial(kernel, capacity, n_dp, n_owner), out_sh...  30 us

profile of v7, /device:TPU:0, one launch (start us, length us, event | category | flops | bytes accessed | tf_op | source)
XLA Modules:
  0.0 30.6 jit_solution(9924107067073558221)
XLA Ops:
  0.0 30.0 %shard_map.37 = f32[1,128]{1,0:T(1,128)S(1)} custom-call(bf16[128,1024]{1,0:T(8,128)(2,1)} %emb_hbm.1, s32[1,128]{1,0:T(1,128)} %bitcast.3, s32[512]{0:T(512)} %pairs_hbm.1), custom_call_target="tpu_custom_call" | custom-call | tf_op jit(solution)/shard_map/pallas_call | solution.py:283
  30.0 0.5 %copy.5 = f32[128]{0:T(128)} copy(f32[128]{0:T(128)S(1)} %bitcast.2) | data formatting | bytes 1024

commit v8 on v7

--- a/solution.py
+++ b/solution.py
@@ -61,7 +61,8 @@
         if k:
             pl.semaphore_signal(barrier, inc=1, device_id=(peers[k], o), device_id_type=MESH)
         pl.semaphore_signal(barrier, inc=1, device_id=(peers[k], o_sib), device_id_type=MESH)
-    pl.semaphore_signal(barrier, inc=1, device_id=(d, o_cpt), device_id_type=MESH)
+    for k in (0,) + NEAR:
+        pl.semaphore_signal(barrier, inc=1, device_id=(peers[k], o_cpt), device_id_type=MESH)
 
     loads[0].wait()
     a = asg[...]
@@ -75,6 +76,79 @@
     count = jnp.dot(t_hot.astype(jnp.bfloat16), before, preferred_element_type=jnp.float32)
     rank = jnp.sum(t_hot * count, axis=0, keepdims=True).astype(jnp.int32)
     slot_iota = lax.broadcasted_iota(jnp.int32, (slots, rows), 0)
+    loads[1].wait()
+    values = emb[...].astype(jnp.float32)
+    unit = (values * lax.rsqrt(jnp.sum(values * values, axis=1, keepdims=True) + 1e-06)).astype(
+        jnp.bfloat16
+    )
+    position = t_row * cap + rank
+    half = n_dp // 2
+    near_base = (d // half) * half
+    cross_base = half - near_base
+    group_iota = lax.broadcasted_iota(jnp.int32, (half * cap, rows), 0)
+
+    def pack(base):
+        place = (group_iota + base * cap == position).astype(jnp.float32).astype(jnp.bfloat16)
+        packed = jnp.dot(place, unit, preferred_element_type=jnp.float32).astype(jnp.bfloat16)
+        send[pl.ds(base, half)] = packed.reshape(half, cap, width)
+
+    pack(near_base)
+    own[d] = send[d]
+
+    pl.semaphore_wait(barrier, 2 * n_dp + len(NEAR))
+
+    def part(h):
+        return pl.ds(0, cap) if h is None else pl.ds(h * (cap // 2), cap // 2)
+
+    def block_copy(k, h=None):
+        p = peers[k]
+        return pltpu.make_async_remote_copy(
+            src_ref=send.at[p, part(h)], dst_ref=own.at[d, part(h)],
+            send_sem=row_ss.at[k, h or 0], recv_sem=row_rs.at[k, h or 0],
+            device_id=(p, o), device_id_type=MESH,
+        )
+
+    def code_copy(k):
+        p = peers[k]
+        return pltpu.make_async_remote_copy(
+            src_ref=code_send.at[p], dst_ref=code_got.at[d], send_sem=id_ss.at[k],
+            recv_sem=id_rs.at[k], device_id=(p, o), device_id_type=MESH,
+        )
+
+    def forward(k, which, h=None):
+        s = peers[k]
+        if which and k in NEAR:
+            src, dst, target = send.at[s], cpt.at[d], (s, o_cpt)
+        else:
+            src, dst = own.at[s, part(h)], (sib, cpt)[which].at[s, part(h)]
+            target = (d, (o_sib, o_cpt)[which])
+        return pltpu.make_async_remote_copy(
+            src_ref=src, dst_ref=dst,
+            send_sem=fw_ss.at[which, k, h or 0], recv_sem=fw_rs.at[which, k, h or 0],
+            device_id=target, device_id_type=MESH,
+        )
+
+    def codes_copy(which):
+        return pltpu.make_async_remote_copy(
+            src_ref=codes.at[0], dst_ref=codes.at[1 + which], send_sem=cd_ss.at[which],
+            recv_sem=cd_rs.at[which], device_id=(d, (o_sib, o_cpt)[which]), device_id_type=MESH,
+        )
+
+    def back(k, which):
+        s = peers[k]
+        return pltpu.make_async_remote_copy(
+            src_ref=res.at[which], dst_ref=ret.at[which, d], send_sem=rt_ss.at[which, k],
+            recv_sem=rt_rs.at[which, k], device_id=(s, (o, o_sib)[which]), device_id_type=MESH,
+        )
+
+    for k in NEAR:
+        block_copy(k).start()
+    forward(0, 1).start()
+    for k in NEAR:
+        forward(k, 1).start()
+    pack(cross_base)
+    for k, h in PIECES[:2]:
+        block_copy(k, h).start()
     lane_hot = (slot_iota == d * cap + rank).astype(jnp.float32)
     slot_codes = lax.dot_general(
         (t_hot * code_row).astype(jnp.bfloat16),
@@ -84,83 +158,15 @@
     )
     for t in range(n_dp):
         code_send[t] = slot_codes[t : t + 1, :]
-
-    loads[1].wait()
-    values = emb[...].astype(jnp.float32)
-    unit = (values * lax.rsqrt(jnp.sum(values * values, axis=1, keepdims=True) + 1e-06)).astype(
-        jnp.bfloat16
-    )
-    position = t_row * cap + rank
-    half = n_dp // 2
-    near_base = (d // half) * half
-    cross_base = half - near_base
-    group_iota = lax.broadcasted_iota(jnp.int32, (half * cap, rows), 0)
-
-    def pack(base):
-        place = (group_iota + base * cap == position).astype(jnp.float32).astype(jnp.bfloat16)
-        packed = jnp.dot(place, unit, preferred_element_type=jnp.float32).astype(jnp.bfloat16)
-        send[pl.ds(base, half)] = packed.reshape(half, cap, width)
-
-    pack(near_base)
-    own[d] = send[d]
     code_got[d] = code_send[d]
-
-    pl.semaphore_wait(barrier, 2 * n_dp)
-
-    def part(h):
-        return pl.ds(0, cap) if h is None else pl.ds(h * (cap // 2), cap // 2)
-
-    def block_copy(k, h=None):
-        p = peers[k]
-        return pltpu.make_async_remote_copy(
-            src_ref=send.at[p, part(h)], dst_ref=own.at[d, part(h)],
-            send_sem=row_ss.at[k, h or 0], recv_sem=row_rs.at[k, h or 0],
-            device_id=(p, o), device_id_type=MESH,
-        )
-
-    def code_copy(k):
-        p = peers[k]
-        return pltpu.make_async_remote_copy(
-            src_ref=code_send.at[p], dst_ref=code_got.at[d], send_sem=id_ss.at[k],
-            recv_sem=id_rs.at[k], device_id=(p, o), device_id_type=MESH,
-        )
-
-    def forward(k, which, h=None):
-        s = peers[k]
-        return pltpu.make_async_remote_copy(
-            src_ref=own.at[s, part(h)], dst_ref=(sib, cpt)[which].at[s, part(h)],
-            send_sem=fw_ss.at[which, k, h or 0], recv_sem=fw_rs.at[which, k, h or 0],
-            device_id=(d, (o_sib, o_cpt)[which]), device_id_type=MESH,
-        )
-
-    def codes_copy(which):
-        return pltpu.make_async_remote_copy(
-            src_ref=codes.at[0], dst_ref=codes.at[1 + which], send_sem=cd_ss.at[which],
-            recv_sem=cd_rs.at[which], device_id=(d, (o_sib, o_cpt)[which]), device_id_type=MESH,
-        )
-
-    def back(k, which):
-        s = peers[k]
-        return pltpu.make_async_remote_copy(
-            src_ref=res.at[which], dst_ref=ret.at[which, d], send_sem=rt_ss.at[which, k],
-            recv_sem=rt_rs.at[which, k], device_id=(s, (o, o_sib)[which]), device_id_type=MESH,
-        )
-
-    for k in NEAR:
-        block_copy(k).start()
-    forward(0, 1).start()
     for k in SEND_ORDER:
         code_copy(k).start()
-    pack(cross_base)
-    for k, h in PIECES[:2]:
-        block_copy(k, h).start()
+    forward(0, 0).start()
     for k in NEAR:
         block_copy(k).wait_recv()
-        forward(k, 1).start()
+        forward(k, 0).start()
         if k == 2:
             block_copy(*PIECES[2]).start()
-    for k in (0,) + NEAR:
-        forward(k, 0).start()
     for k in NEAR + CROSS:
         code_copy(k).wait_recv()
     codes[0] = jnp.sum(code_got[...], axis=0)

time: 30.7 us -> 33.2 us (1.081)
  Pallas kernels: 30 us -> 32.6 us
    pallas_call x1, Pallas kernels: 30 us -> 32.6 us  [fused(): pl.pallas_call(functools.partial(kernel, capacity, n_dp, n_owner), out_sh...]
where the time goes in v8:
time: 33.2 us; the launch traced here: 33.1 us
  Pallas kernels  32.6 us (98%)
  local copies, waits for them, and re-layouts  0.51 us (2%)
    pallas_call x1, Pallas kernels, fused(): pl.pallas_call(functools.partial(kernel, capacity, n_dp, n_owner), out_sh...  32.6 us

profile of v8, /device:TPU:0, one launch (start us, length us, event | category | flops | bytes accessed | tf_op | source)
XLA Modules:
  0.0 33.1 jit_solution(2908275157117452690)
XLA Ops:
  0.0 32.6 %shard_map.37 = f32[1,128]{1,0:T(1,128)S(1)} custom-call(bf16[128,1024]{1,0:T(8,128)(2,1)} %emb_hbm.1, s32[1,128]{1,0:T(1,128)} %bitcast.3, s32[512]{0:T(512)} %pairs_hbm.1), custom_call_target="tpu_custom_call" | custom-call | tf_op jit(solution)/shard_map/pallas_call | solution.py:289
  32.6 0.5 %copy.5 = f32[128]{0:T(128)} copy(f32[128]{0:T(128)S(1)} %bitcast.2) | data formatting | bytes 1024

commit v9 on v8

--- a/solution.py
+++ b/solution.py
@@ -61,8 +61,7 @@
         if k:
             pl.semaphore_signal(barrier, inc=1, device_id=(peers[k], o), device_id_type=MESH)
         pl.semaphore_signal(barrier, inc=1, device_id=(peers[k], o_sib), device_id_type=MESH)
-    for k in (0,) + NEAR:
-        pl.semaphore_signal(barrier, inc=1, device_id=(peers[k], o_cpt), device_id_type=MESH)
+    pl.semaphore_signal(barrier, inc=1, device_id=(d, o_cpt), device_id_type=MESH)
 
     loads[0].wait()
     a = asg[...]
@@ -95,7 +94,7 @@
     pack(near_base)
     own[d] = send[d]
 
-    pl.semaphore_wait(barrier, 2 * n_dp + len(NEAR))
+    pl.semaphore_wait(barrier, 2 * n_dp)
 
     def part(h):
         return pl.ds(0, cap) if h is None else pl.ds(h * (cap // 2), cap // 2)
@@ -117,15 +116,10 @@
 
     def forward(k, which, h=None):
         s = peers[k]
-        if which and k in NEAR:
-            src, dst, target = send.at[s], cpt.at[d], (s, o_cpt)
-        else:
-            src, dst = own.at[s, part(h)], (sib, cpt)[which].at[s, part(h)]
-            target = (d, (o_sib, o_cpt)[which])
-        return pltpu.make_async_remote_copy(
-            src_ref=src, dst_ref=dst,
+        return pltpu.make_async_remote_copy(
+            src_ref=own.at[s, part(h)], dst_ref=(sib, cpt)[which].at[s, part(h)],
             send_sem=fw_ss.at[which, k, h or 0], recv_sem=fw_rs.at[which, k, h or 0],
-            device_id=target, device_id_type=MESH,
+            device_id=(d, (o_sib, o_cpt)[which]), device_id_type=MESH,
         )
 
     def codes_copy(which):
@@ -144,8 +138,6 @@
     for k in NEAR:
         block_copy(k).start()
     forward(0, 1).start()
-    for k in NEAR:
-        forward(k, 1).start()
     pack(cross_base)
     for k, h in PIECES[:2]:
         block_copy(k, h).start()
@@ -161,12 +153,13 @@
     code_got[d] = code_send[d]
     for k in SEND_ORDER:
         code_copy(k).start()
-    forward(0, 0).start()
     for k in NEAR:
         block_copy(k).wait_recv()
-        forward(k, 0).start()
+        forward(k, 1).start()
         if k == 2:
             block_copy(*PIECES[2]).start()
+    for k in (0,) + NEAR:
+        forward(k, 0).start()
     for k in NEAR + CROSS:
         code_copy(k).wait_recv()
     codes[0] = jnp.sum(code_got[...], axis=0)

time: 33.2 us -> 30.7 us (0.925)
  Pallas kernels: 32.6 us -> 30 us
    pallas_call x1, Pallas kernels: 32.6 us -> 30 us  [fused(): pl.pallas_call(functools.partial(kernel, capacity, n_dp, n_owner), out_sh...]
where the time goes in v9:
time: 30.7 us; the launch traced here: 30.6 us
  Pallas kernels  30 us (98%)
  local copies, waits for them, and re-layouts  0.51 us (2%)
    pallas_call x1, Pallas kernels, fused(): pl.pallas_call(functools.partial(kernel, capacity, n_dp, n_owner), out_sh...  30 us

profile of v9, /device:TPU:0, one launch (start us, length us, event | category | flops | bytes accessed | tf_op | source)
XLA Modules:
  0.0 30.6 jit_solution(4384132646163147401)
XLA Ops:
  0.0 30.0 %shard_map.37 = f32[1,128]{1,0:T(1,128)S(1)} custom-call(bf16[128,1024]{1,0:T(8,128)(2,1)} %emb_hbm.1, s32[1,128]{1,0:T(1,128)} %bitcast.3, s32[512]{0:T(512)} %pairs_hbm.1), custom_call_target="tpu_custom_call" | custom-call | tf_op jit(solution)/shard_map/pallas_call | solution.py:282
  30.1 0.5 %copy.5 = f32[128]{0:T(128)} copy(f32[128]{0:T(128)S(1)} %bitcast.2) | data formatting | bytes 1024

commit v10 on v7

--- a/solution.py
+++ b/solution.py
@@ -152,13 +152,13 @@
     for k in SEND_ORDER:
         code_copy(k).start()
     pack(cross_base)
-    for k, h in PIECES[:2]:
+    for k, h in PIECES[:1]:
         block_copy(k, h).start()
     for k in NEAR:
         block_copy(k).wait_recv()
         forward(k, 1).start()
-        if k == 2:
-            block_copy(*PIECES[2]).start()
+        if k != 2:
+            block_copy(*PIECES[(k + 1) // 2]).start()
     for k in (0,) + NEAR:
         forward(k, 0).start()
     for k in NEAR + CROSS:

time: 30.7 us -> 31.5 us (1.026)
  Pallas kernels: 30 us -> 30.8 us
    pallas_call x1, Pallas kernels: 30 us -> 30.8 us  [fused(): pl.pallas_call(functools.partial(kernel, capacity, n_dp, n_owner), out_sh...]
where the time goes in v10:
time: 31.5 us; the launch traced here: 31.4 us
  Pallas kernels  30.8 us (98%)
  local copies, waits for them, and re-layouts  0.51 us (2%)
    pallas_call x1, Pallas kernels, fused(): pl.pallas_call(functools.partial(kernel, capacity, n_dp, n_owner), out_sh...  30.8 us

profile of v10, /device:TPU:0, one launch (start us, length us, event | category | flops | bytes accessed | tf_op | source)
XLA Modules:
  0.0 31.4 jit_solution(1963911595296187517)
XLA Ops:
  0.0 30.8 %shard_map.37 = f32[1,128]{1,0:T(1,128)S(1)} custom-call(bf16[128,1024]{1,0:T(8,128)(2,1)} %emb_hbm.1, s32[1,128]{1,0:T(1,128)} %bitcast.3, s32[512]{0:T(512)} %pairs_hbm.1), custom_call_target="tpu_custom_call" | custom-call | tf_op jit(solution)/shard_map/pallas_call | solution.py:283
  30.8 0.5 %copy.5 = f32[128]{0:T(128)} copy(f32[128]{0:T(128)S(1)} %bitcast.2) | data formatting | bytes 1024
